TPU v7x, 32 devices: a whole 2x2x4 slice. The times are simulated.
32 devices in a mesh: frame: 4 (over y, x), tile: 8 (over z, core).
Axes of the slice: x: 2, y: 2, z: 4, core: 2. Of those that a mesh axis runs over, the one named last changes fastest.
Arguments:
- latents: bfloat16 [4, 320, 2048], P('frame', None, 'tile'), may hold values from -80 to 80
- out_grad: bfloat16 [4, 320, 2048], P('frame', None, 'tile'), may hold values from -6 to 6
- w_spatial: bfloat16 [320, 2880], P('tile', 'frame'), may hold values from -0.109375 to 0.109375
- w_temporal: bfloat16 [320, 960], P('tile', 'frame'), may hold values from -0.1875 to 0.1875
- norm_gain: float32 [320], replicated, may hold values from 0.5 to 1.5
- norm_shift: float32 [320], replicated, may hold values from -1 to 1
- heights: int32 [8], P('tile'), may hold values from 8 to 16, as said below
Outputs:
- grad_input: bfloat16 [4, 320, 2048], P('frame', None, 'tile')
- grad_spatial: float32 [320, 2880], P('tile', 'frame')
- grad_temporal: float32 [320, 960], P('tile', 'frame')
- grad_gain: float32 [320], replicated
- grad_shift: float32 [320], replicated
Inputs may be any that keep to these rules, and one draw needn't show every extreme that they name: `heights`: each entry is a multiple of 8; in every draw at least one strip has 16 live rows.
All inputs are finite; a program needn't handle non-finite values.
Results may differ from a plain program's by a relative error of at most 0.028.
Values may be sent and summed in bfloat16 or wider, within the bound.
A program may use at most 64 MiB of HBM per device.

v0:
```python
import jax
import jax.numpy as jnp
from jax import lax
from jax.experimental import pallas as pl
from jax.experimental.pallas import tpu as pltpu
from jax.sharding import PartitionSpec as P

GROUPS = 32
COLUMNS = 16
STRIP_ROWS = 16


EPSILON = 1e-05


def from_behind(shard, axis, by):
    peers = lax.axis_size(axis)
    pairs = [(i, i + by) for i in range(peers) if 0 <= i + by < peers]
    return lax.ppermute(shard, axis, pairs)


def padded_2(cells, sides, width):
    for axis, dim in sides:
        count = lax.axis_size(axis)
        ends = count - 1
        head = lax.slice_in_dim(cells, 0, width, axis=dim)
        tail = lax.slice_in_dim(cells, cells.shape[dim] - width, cells.shape[dim], axis=dim)
        cells = jnp.concatenate(
            [
                lax.ppermute(tail, axis, [(i, (i + 1) % count) for i in range(ends)]),
                cells,
                lax.ppermute(head, axis, [((i + 1) % count, i) for i in range(ends)]),
            ],
            axis=dim,
        )
    return cells


def flip_taps(weight, tap_count):
    outputs = weight.shape[0]
    return jnp.transpose(weight.reshape(outputs, tap_count, -1)[:, ::-1, :], (2, 1, 0)).reshape(
        -1, tap_count * outputs
    )


def padded_rows(row_grid, above_row, below_row, height):
    channel_count = row_grid.shape[0]
    padded = jnp.zeros((channel_count, STRIP_ROWS + 2, COLUMNS + 2), row_grid.dtype)
    padded = padded.at[:, 1 : STRIP_ROWS + 1, 1 : COLUMNS + 1].set(row_grid)
    padded = padded.at[:, 0, 1 : COLUMNS + 1].set(above_row)
    below_block = jnp.pad(below_row, ((0, 0), (1, 1)))[:, None, :]
    return lax.dynamic_update_slice(padded, below_block, (jnp.int32(0), height + 1, jnp.int32(0)))


def tap_columns(padded, row_count):
    pieces = [
        padded[:, row_step : row_step + row_count, col_step : col_step + COLUMNS]
        for row_step in range(3)
        for col_step in range(3)
    ]
    return jnp.stack(pieces, axis=0).reshape(9 * padded.shape[0], row_count * COLUMNS)


def local(latents, out_grad, w_spatial, w_temporal, norm_gain, norm_shift, heights):
    channel_count = latents.shape[1]
    cell_count = latents.shape[2]
    group_size = channel_count // GROUPS
    height = heights[0]
    slot_row = jnp.arange(cell_count, dtype=jnp.int32) // COLUMNS
    live_cells = slot_row < height
    live_float = live_cells.astype(jnp.float32)
    contract_last = (((1,), (1,)), ((), ()))
    part_spatial_w, part_temporal_w = (
        lax.all_gather(w_spatial, "frame", axis=1, tiled=True),
        lax.all_gather(w_temporal, "frame", axis=1, tiled=True),
    )
    spatial_full, temporal_full = (
        lax.all_gather(part_spatial_w, "tile", axis=0, tiled=True),
        lax.all_gather(part_temporal_w, "tile", axis=0, tiled=True),
    )
    latent_full = latents[0].astype(jnp.float32)
    masked = latent_full * live_float[None, :]
    group_sum = masked.reshape(GROUPS, group_size, cell_count).sum(axis=(1, 2))
    group_square = (masked * latent_full).reshape(GROUPS, group_size, cell_count).sum(axis=(1, 2))
    own_count = height.astype(jnp.float32) * COLUMNS
    total_sum, total_square, position_count = lax.psum(
        (group_sum, group_square, own_count), ("frame", "tile")
    )
    group_count = position_count * group_size
    group_mean = total_sum / group_count
    group_rstd = lax.rsqrt(total_square / group_count - group_mean * group_mean + EPSILON)
    mean_column = jnp.repeat(group_mean, group_size)[:, None]
    rstd_column = jnp.repeat(group_rstd, group_size)[:, None]
    gain_column = norm_gain[:, None]
    normed = (latent_full - mean_column) * rstd_column
    pre_act = gain_column * normed + norm_shift[:, None]
    activated = jnp.where(live_cells[None, :], jax.nn.silu(pre_act), 0.0).astype(jnp.bfloat16)
    act_grid = activated.reshape(channel_count, STRIP_ROWS, COLUMNS)
    last_live = lax.dynamic_slice_in_dim(act_grid, height - 1, 1, 1)[:, 0, :]
    from_above = from_behind(last_live, "tile", 1)
    from_below = from_behind(act_grid[:, 0, :], "tile", -1)
    act_padded = padded_rows(act_grid, from_above, from_below, height)
    act_columns = tap_columns(act_padded, STRIP_ROWS)
    spatial_raw = jnp.dot(spatial_full, act_columns, preferred_element_type=jnp.float32)
    spatial_out = jnp.where(live_cells[None, :], spatial_raw, 0.0).astype(jnp.bfloat16)
    spatial_frames = padded_2(spatial_out[None], (("frame", 0),), 1)
    grad_here = jnp.where(live_cells[None, :], out_grad[0], jnp.zeros((), jnp.bfloat16))
    grad_frames = padded_2(grad_here[None], (("frame", 0),), 1)
    part_temporal = lax.dot_general(
        grad_here,
        spatial_frames.reshape(3 * channel_count, cell_count),
        contract_last,
        preferred_element_type=jnp.float32,
    )
    grad_spat = jnp.dot(
        flip_taps(temporal_full, 3),
        grad_frames.reshape(3 * channel_count, cell_count),
        preferred_element_type=jnp.float32,
    )
    grad_spat = jnp.where(live_cells[None, :], grad_spat, 0.0).astype(jnp.bfloat16)
    spat_grid = grad_spat.reshape(channel_count, STRIP_ROWS, COLUMNS)
    grad_last = lax.dynamic_slice_in_dim(spat_grid, height - 1, 1, 1)[:, 0, :]
    grad_above = from_behind(grad_last, "tile", 1)
    grad_below = from_behind(spat_grid[:, 0, :], "tile", -1)
    grad_padded = padded_rows(spat_grid, grad_above, grad_below, height)
    spatial_flip = flip_taps(spatial_full, 9)
    grad_act = jnp.dot(
        spatial_flip, tap_columns(grad_padded, STRIP_ROWS), preferred_element_type=jnp.float32
    )
    part_spatial = lax.dot_general(
        grad_spat, act_columns, contract_last, preferred_element_type=jnp.float32
    )
    sigmoid_act = jax.nn.sigmoid(pre_act)
    grad_pre = jnp.where(
        live_cells[None, :], grad_act * sigmoid_act * (1.0 + pre_act * (1.0 - sigmoid_act)), 0.0
    )
    chan_gain, chan_shift = lax.psum(
        (jnp.sum(grad_pre * normed, axis=1), jnp.sum(grad_pre, axis=1)), ("frame", "tile")
    )
    shift_sum = (norm_gain * chan_shift).reshape(GROUPS, group_size).sum(1) / group_count
    gain_sum = (norm_gain * chan_gain).reshape(GROUPS, group_size).sum(1) / group_count
    result = grad_here.astype(jnp.float32) + rstd_column * (
        gain_column * grad_pre
        - jnp.repeat(shift_sum, group_size)[:, None]
        - normed * jnp.repeat(gain_sum, group_size)[:, None]
    )
    grad_input = jnp.where(live_cells[None, :], result, 0.0).astype(jnp.bfloat16)[None]
    tile_spatial, tile_temporal = (
        lax.psum_scatter(
            part_spatial.astype(jnp.bfloat16), "tile", scatter_dimension=0, tiled=True
        ).astype(jnp.float32),
        lax.psum_scatter(
            part_temporal.astype(jnp.bfloat16), "tile", scatter_dimension=0, tiled=True
        ).astype(jnp.float32),
    )
    grad_spatial, grad_temporal = (
        lax.psum_scatter(
            tile_spatial.astype(jnp.bfloat16), "frame", scatter_dimension=1, tiled=True
        ).astype(jnp.float32),
        lax.psum_scatter(
            tile_temporal.astype(jnp.bfloat16), "frame", scatter_dimension=1, tiled=True
        ).astype(jnp.float32),
    )
    grad_scale = lax.rsqrt(position_count)
    return (
        grad_input,
        grad_scale * grad_spatial,
        grad_scale * grad_temporal,
        grad_scale * chan_gain,
        grad_scale * chan_shift,
    )


MESH = pl.DeviceIdType.MESH
BF = jnp.bfloat16
F32 = jnp.float32


def iota(shape, dim):
    return lax.broadcasted_iota(jnp.int32, shape, dim)


def row_of(column):
    n = column.shape[0]
    eye = iota((n, n), 0) == iota((n, n), 1)
    return jnp.sum(jnp.where(eye, column, 0.0), axis=0, keepdims=True)


def column_of(row):
    n = row.shape[1]
    eye = iota((n, n), 0) == iota((n, n), 1)
    return jnp.sum(jnp.where(eye, row, 0.0), axis=1, keepdims=True)


def group_column(row, size):
    n = row.shape[1]
    steps = 1 << 11
    factor = steps // size + 1
    same = (iota((n, n), 0) * factor) // steps == (iota((n, n), 1) * factor) // steps
    return jnp.sum(jnp.where(same, row, 0.0), axis=1, keepdims=True)


def whole_kernel(
    lat, og, ws, wt, gain, shift, heights,
    gi, dws, dwt, dgain, dshift,
    g_t, g_a, g_b, p_t, p_a, p_b,
    r0t, r0a, r0b, r1t, r1a, r1b, r2t, r2a, r2b, r3t, r3a, r3b, r4t, r4a, r4b,
    xs_t, xs_a, xs_b, xr_t, xr_a, xr_b, ys_t, ys_a, ys_b, yr_t, yr_a, yr_b,
    ogf, sof, hsend, hrecv, ext, cols, zbuf, acc, normed_ref, pre_ref, gs_ref, gpre_ref,
    msg, tbuf, fbuf,
    ag_send, ag_recv, rs_send, rs_recv, fr_send, fr_recv, ha_send, ha_recv, st_send, st_recv, tr_send, tr_recv,
):
    frames, tiles = 4, 8
    chans, cells = lat.shape
    own = ws.shape[0]
    lanes = tuple(buf.shape[4] for buf in (g_t, g_a, g_b))
    rows_in = 2 * own
    sp = 2 * (lanes[1] + lanes[2])
    tp = 2 * lanes[0]
    gathered, partial = (g_t, g_a, g_b), (p_t, p_a, p_b)
    landing = (
        (r0t, r0a, r0b), (r1t, r1a, r1b), (r2t, r2a, r2b), (r3t, r3a, r3b), (r4t, r4a, r4b),
    )
    sw, tw = ws.shape[1], wt.shape[1]
    group = chans // GROUPS
    f = lax.axis_index("frame")
    t = lax.axis_index("tile")
    y, x = f // 2, f % 2
    z, c = t // 2, t % 2
    zh, zl = z // 2, z % 2
    h = heights[0]
    live = iota((1, cells), 1) < h * COLUMNS
    short = h < STRIP_ROWS

    x_peer = (y * 2 + (1 - x), t)
    y_peer = ((1 - y) * 2 + x, t)
    z0_peer = (f, (zh * 2 + (1 - zl)) * 2 + c)
    z1_peer = (f, ((1 - zh) * 2 + zl) * 2 + c)
    c_peer = (f, z * 2 + (1 - c))

    barrier = pltpu.get_barrier_semaphore()
    for d in range(1, tiles):
        pl.semaphore_signal(barrier, inc=1, device_id=(f, (t + d) % tiles), device_id_type=MESH)
    for d in range(1, frames):
        pl.semaphore_signal(barrier, inc=1, device_id=((f + d) % frames, t), device_id_type=MESH)

    q_own = jnp.where(zh == 0, y, x)
    p_own = jnp.where(zh == 0, x, y)
    slot_own = q_own * 4 + p_own * 2 + zl
    def halves(src, wide):
        w32 = src[...].astype(F32)
        w32 = jnp.concatenate([w32, jnp.zeros((own, wide - w32.shape[1]), F32)], axis=1)
        first, second = w32[:, : wide // 2], w32[:, wide // 2 :]
        return jnp.where(c == 0, first, second), jnp.where(c == 0, second, first)

    kept_t, sent_t = halves(wt, tp)
    kept_s, sent_s = halves(ws, sp)
    kept = (kept_t, kept_s[:, : lanes[1]], kept_s[:, lanes[1] :])
    sent = (sent_t, sent_s[:, : lanes[1]], sent_s[:, lanes[1] :])

    def staged(ref, rows):
        ref[...] = jnp.concatenate(
            [rows, jnp.zeros((ref.shape[0] - own, rows.shape[1]), F32)], axis=0
        ).astype(BF)

    for ref, rows in zip((xs_t, xs_a, xs_b), sent):
        staged(ref, rows)
    pl.semaphore_wait(barrier, tiles + frames - 2)

    pending = []

    def remote(src, dst, ss, rs, peer):
        copy = pltpu.make_async_remote_copy(
            src_ref=src, dst_ref=dst, send_sem=ss, recv_sem=rs, device_id=peer, device_id_type=MESH
        )
        copy.start()
        pending.append(copy)
        return copy

    def trade(which, kind, src, dst):
        return [
            remote(src, dst, tr_send.at[which, kind], tr_recv.at[which, kind], c_peer)
        ]

    def gather_step(kind, step):
        buf = gathered[kind]
        if step == 0:
            moves = [(0, (c, zh, pl.ds(slot_own, 1)), z1_peer)]
        elif step == 1:
            moves = [
                (1, (c, 0, pl.ds(y * 4 + x * 2 + zl, 1)), z0_peer),
                (2, (c, 1, pl.ds(x * 4 + y * 2 + zl, 1)), z0_peer),
            ]
        elif step == 2:
            moves = [
                (3, (c, 0, pl.ds(y * 4 + x * 2, 2)), x_peer),
                (4, (c, 1, pl.ds(x * 4 + y * 2, 2)), y_peer),
            ]
        elif step == 3:
            moves = [
                (5, (c, 0, pl.ds(y * 4, 4)), y_peer),
                (6, (c, 1, pl.ds(x * 4, 4)), x_peer),
            ]
        else:
            moves = [(7, (c,), c_peer)]
        return [
            remote(buf.at[at], buf.at[at], ag_send.at[kind, i], ag_recv.at[kind, i], peer)
            for i, at, peer in moves
        ]

    def arrived(copies):
        for copy in copies:
            copy.wait_recv()

    def frame_copies(src, prev_dst, next_dst, base):
        up = pltpu.make_async_remote_copy(
            src_ref=src, dst_ref=prev_dst, send_sem=fr_send.at[base], recv_sem=fr_recv.at[base],
            device_id=((f + 1) % frames, t), device_id_type=MESH,
        )
        down = pltpu.make_async_remote_copy(
            src_ref=src, dst_ref=next_dst, send_sem=fr_send.at[base + 1], recv_sem=fr_recv.at[base + 1],
            device_id=((f + frames - 1) % frames, t), device_id_type=MESH,
        )
        return up, down

    def frame_start(pair):
        pl.when(f < frames - 1)(lambda: pair[0].start())
        pl.when(f > 0)(lambda: pair[1].start())

    def frame_arrived(pair):
        pl.when(f > 0)(lambda: pair[0].wait_recv())
        pl.when(f < frames - 1)(lambda: pair[1].wait_recv())

    def frame_sent(pair):
        pl.when(f < frames - 1)(lambda: pair[0].wait_send())
        pl.when(f > 0)(lambda: pair[1].wait_send())

    def strip_copies(which):
        down = pltpu.make_async_remote_copy(
            src_ref=hsend.at[which, 0], dst_ref=hrecv.at[which, 0],
            send_sem=ha_send.at[which, 0], recv_sem=ha_recv.at[which, 0],
            device_id=(f, (t + 1) % tiles), device_id_type=MESH,
        )
        up = pltpu.make_async_remote_copy(
            src_ref=hsend.at[which, 1], dst_ref=hrecv.at[which, 1],
            send_sem=ha_send.at[which, 1], recv_sem=ha_recv.at[which, 1],
            device_id=(f, (t + tiles - 1) % tiles), device_id_type=MESH,
        )
        return down, up

    def strip_start(pair, which, grid):
        half = cells // 2
        hsend[which, 0] = jnp.where(short, grid[:, :half], grid[:, half:]).astype(BF)
        hsend[which, 1] = grid[:, :half].astype(BF)
        pl.when(t < tiles - 1)(lambda: pair[0].start())
        pl.when(t > 0)(lambda: pair[1].start())

    def strip_arrived(pair):
        pl.when(t > 0)(lambda: pair[0].wait_recv())
        pl.when(t < tiles - 1)(lambda: pair[1].wait_recv())

    def strip_sent(pair):
        pl.when(t < tiles - 1)(lambda: pair[0].wait_send())
        pl.when(t > 0)(lambda: pair[1].wait_send())

    def strip_extended(which, grid):
        half = cells // 2
        above = hrecv[which, 0].astype(F32)
        below = hrecv[which, 1].astype(F32)
        return jnp.concatenate(
            [above, grid[:, :half], jnp.where(short, below, grid[:, half:]), below], axis=1
        )

    stride = msg.shape[3] // 3

    def sums_start(which, rows):
        row = jnp.zeros((1, msg.shape[3]), F32)
        for i, part in enumerate(rows):
            at = i * stride
            row_parts = [jnp.zeros((1, at), F32)] if at else []
            row_parts.append(part)
            rest = msg.shape[3] - at - part.shape[1]
            if rest:
                row_parts.append(jnp.zeros((1, rest), F32))
            row = row + jnp.concatenate(row_parts, axis=1)
        msg[which, 0] = row
        tbuf[which, t] = msg[which, 0]
        return [
            remote(
                msg.at[which, 0], tbuf.at[which, t], st_send.at[which, d], st_recv.at[which, d],
                (f, (t + d) % tiles),
            )
            for d in range(1, tiles)
        ]

    def sums_middle(which, copies):
        arrived(copies)
        total = tbuf[which, 0]
        for i in range(1, tiles):
            total = total + tbuf[which, i]
        msg[which, 1] = total
        fbuf[which, f] = total
        return [
            remote(
                msg.at[which, 1], fbuf.at[which, f], st_send.at[which, tiles + d],
                st_recv.at[which, tiles + d], ((f + d) % frames, t),
            )
            for d in range(1, frames)
        ]

    def sums_end(which, copies):
        arrived(copies)
        total = fbuf[which, 0]
        for i in range(1, frames):
            total = total + fbuf[which, i]
        return total

    traded = [
        trade(0, kind, src, dst)
        for kind, (src, dst) in enumerate(((xs_t, xr_t), (xs_a, xr_a), (xs_b, xr_b)))
    ]
    og_pair = frame_copies(og, ogf.at[0], ogf.at[1], 0)
    frame_start(og_pair)

    @pl.when(f == 0)
    def _():
        ogf[0] = jnp.zeros_like(ogf[0])
        sof[0:chans] = jnp.zeros((chans, cells), BF)

    @pl.when(f == frames - 1)
    def _():
        ogf[1] = jnp.zeros_like(ogf[1])
        sof[2 * chans : 3 * chans] = jnp.zeros((chans, cells), BF)

    @pl.when(t == 0)
    def _():
        hrecv[0, 0] = jnp.zeros_like(hrecv[0, 0])
        hrecv[1, 0] = jnp.zeros_like(hrecv[1, 0])

    @pl.when(t == tiles - 1)
    def _():
        hrecv[0, 1] = jnp.zeros_like(hrecv[0, 1])
        hrecv[1, 1] = jnp.zeros_like(hrecv[1, 1])

    sof[3 * chans :] = jnp.zeros((sof.shape[0] - 3 * chans, cells), BF)
    cols[9 * chans :] = jnp.zeros((cols.shape[0] - 9 * chans, cells), BF)

    lat32 = lat[...].astype(F32)
    masked = jnp.where(live, lat32, 0.0)
    count_row = jnp.zeros((1, 128), F32) + h.astype(F32) * COLUMNS
    stat = sums_start(
        0,
        [
            row_of(jnp.sum(masked, axis=1, keepdims=True)),
            row_of(jnp.sum(masked * masked, axis=1, keepdims=True)),
            count_row,
        ],
    )
    chain = [None] * 3
    for kind, ref in enumerate((xr_t, xr_a, xr_b)):
        arrived(traded[kind])
        other = ref[0:own].astype(F32)
        gathered[kind][c, zh, slot_own] = jnp.concatenate(
            [jnp.where(c == 0, kept[kind], other), jnp.where(c == 0, other, kept[kind])], axis=0
        ).astype(BF)
        chain[kind] = gather_step(kind, 0)

    def forth(kind, step):
        arrived(chain[kind])
        if step < 5:
            chain[kind] = gather_step(kind, step)

    forth(0, 1)
    stat = sums_middle(0, stat)
    forth(1, 1)
    forth(2, 1)
    forth(0, 2)
    total = sums_end(0, stat)
    count = total[:, 2 * stride : 2 * stride + 1]
    group_count = count * group
    gain_row = gain[...].reshape(1, chans)
    gain_column = column_of(gain_row)
    shift_column = column_of(shift[...].reshape(1, chans))
    mean = group_column(total[:, 0:chans], group) / group_count
    rstd = lax.rsqrt(
        group_column(total[:, stride : stride + chans], group) / group_count - mean * mean + EPSILON
    )
    normed = (lat[...].astype(F32) - mean) * rstd
    pre = gain_column * normed + shift_column
    normed_ref[...] = normed
    pre_ref[...] = pre
    act = jnp.where(live, pre * jax.nn.sigmoid(pre), 0.0).astype(BF).astype(F32)
    act_pair = strip_copies(0)
    strip_start(act_pair, 0, act)
    forth(1, 2)
    forth(0, 3)
    forth(2, 2)
    frame_arrived(og_pair)
    og_here = jnp.where(live, og[...], jnp.zeros((), BF))
    og_next = jnp.where(live, ogf[1], jnp.zeros((), BF))
    og_prev = jnp.where(live, ogf[0], jnp.zeros((), BF))
    forth(1, 3)
    forth(0, 4)
    forth(2, 3)
    strip_arrived(act_pair)
    ext[...] = strip_extended(0, act)

    width = ext.shape[1]
    chunk = 64
    col = iota((1, cells), 1) % COLUMNS
    left_ok = col >= 1
    right_ok = col < COLUMNS - 1
    half = cells // 2

    def cut(rolled, b):
        piece = rolled[:, half : half + cells]
        if b < 0:
            piece = jnp.where(left_ok, piece, 0.0)
        if b > 0:
            piece = jnp.where(right_ok, piece, 0.0)
        return piece

    def tap_rows(i, carry):
        r = pl.multiple_of(i * chunk, chunk)
        rows = ext[pl.ds(r, chunk)]
        for k in range(9):
            a, b = k // 3 - 1, k % 3 - 1
            s = a * COLUMNS + b
            rolled = pltpu.roll(rows, (-s) % width, 1) if s else rows
            cols[pl.ds(pl.multiple_of(k * chans + r, 64), chunk)] = cut(rolled, b).astype(BF)
        return carry

    lax.fori_loop(0, chans // chunk, tap_rows, 0)

    def slots(fi):
        yi, xi = fi // 2, fi % 2
        return yi * 4 + xi * 2, xi * 4 + yi * 2

    def weight(bufs, fi):
        at = slots(fi)
        sides = []
        for side in range(2):
            for buf in bufs:
                sides.append(
                    jnp.concatenate(
                        [buf[side, zi // 2, at[zi // 2] + zi % 2] for zi in range(4)], axis=0
                    )
                )
        return jnp.concatenate(sides, axis=1)

    def put(bufs, fi, value):
        at = slots(fi)
        lane = 0
        for side in range(2):
            for buf in bufs:
                wide = buf.shape[4]
                for zi in range(4):
                    buf[side, zi // 2, at[zi // 2] + zi % 2] = value[
                        zi * rows_in : (zi + 1) * rows_in, lane : lane + wide
                    ].astype(BF)
                lane += wide

    contract_first = (((0,), (0,)), ((), ()))
    contract_last = (((1,), (1,)), ((), ()))

    forth(0, 5)
    windows = (og_next, og_here, og_prev)
    for fi in range(frames):
        block = weight((g_t,), fi)
        lo, hi = fi * tw, (fi + 1) * tw
        for k in range(3):
            first, last = max(lo, k * chans), min(hi, (k + 1) * chans)
            if first < last:
                part = lax.dot_general(
                    block, windows[k], contract_first, preferred_element_type=F32
                )
                zbuf[first:last, 0:cells] = part[first - lo : last - lo]
    gs = zbuf[0:chans, 0:cells] + zbuf[chans : 2 * chans, 0:cells]
    gs = gs + zbuf[2 * chans : 3 * chans, 0:cells]
    gs = jnp.where(live, gs, 0.0).astype(BF).astype(F32)
    gs_ref[...] = gs
    gs_pair = strip_copies(1)
    strip_start(gs_pair, 1, gs)

    def spatial_terms(fi, carry):
        here = gs_ref[...].astype(BF)
        piece = cols[pl.ds(pl.multiple_of(fi * sw, 16), sp)]
        put((p_a, p_b), fi, lax.dot_general(here, piece, contract_last, preferred_element_type=F32))
        return carry

    lax.fori_loop(0, frames, spatial_terms, 0)

    def reduce_step(kind, step):
        buf = partial[kind]
        into = landing[step][kind]
        if step == 0:
            moves = [(0, (1 - c,), into, c_peer)]
        elif step == 1:
            moves = [
                (1, (c, 0, pl.ds((1 - y) * 4, 4)), into.at[0], y_peer),
                (2, (c, 1, pl.ds((1 - x) * 4, 4)), into.at[1], x_peer),
            ]
        elif step == 2:
            moves = [
                (3, (c, 0, pl.ds(y * 4 + (1 - x) * 2, 2)), into.at[0], x_peer),
                (4, (c, 1, pl.ds(x * 4 + (1 - y) * 2, 2)), into.at[1], y_peer),
            ]
        elif step == 3:
            moves = [
                (5, (c, 0, pl.ds(y * 4 + x * 2 + (1 - zl), 1)), into.at[0], z0_peer),
                (6, (c, 1, pl.ds(x * 4 + y * 2 + (1 - zl), 1)), into.at[1], z0_peer),
            ]
        else:
            q = jnp.where(zh == 0, x, y)
            p = jnp.where(zh == 0, y, x)
            moves = [(7, (c, 1 - zh, pl.ds(q * 4 + p * 2 + zl, 1)), into, z1_peer)]
        return [
            remote(buf.at[at], dst, rs_send.at[kind, i], rs_recv.at[kind, i], peer)
            for i, at, dst, peer in moves
        ]

    def reduce_add(kind, step):
        buf = partial[kind]
        into = landing[step][kind]
        blocks = (8, 4, 2, 1)[step]
        starts = (
            (0, 0),
            (y * 4, x * 4),
            (y * 4 + x * 2, x * 4 + y * 2),
            (y * 4 + x * 2 + zl, x * 4 + y * 2 + zl),
        )[step]
        for hi in range(2):
            def add(i, carry):
                here = buf[c, hi, starts[hi] + i].astype(F32) + into[hi, i].astype(F32)
                buf[c, hi, starts[hi] + i] = here.astype(BF)
                return carry

            lax.fori_loop(0, blocks, add, 0)

    back = [None] * 3

    def reduce_start(kind):
        back[kind] = reduce_step(kind, 0)

    def reduce_on(kind, step):
        arrived(back[kind])
        reduce_add(kind, step - 1)
        back[kind] = reduce_step(kind, step)

    forth(1, 4)
    forth(2, 4)
    reduce_start(1)
    reduce_start(2)
    strip_arrived(gs_pair)
    ext[...] = strip_extended(1, gs_ref[...])
    forth(1, 5)
    forth(2, 5)
    reduce_on(1, 1)

    acc[...] = jnp.zeros_like(acc)

    def forward(fi, carry):
        piece = cols[pl.ds(pl.multiple_of(fi * sw, 16), sp)]
        acc[...] += jnp.dot(weight((g_a, g_b), fi), piece, preferred_element_type=F32)
        return carry

    lax.fori_loop(0, frames, forward, 0)
    spatial_out = jnp.where(live, acc[...], 0.0).astype(BF)
    sof[chans : 2 * chans] = spatial_out
    so_pair = frame_copies(
        sof.at[pl.ds(chans, chans)], sof.at[pl.ds(0, chans)], sof.at[pl.ds(2 * chans, chans)], 2
    )
    frame_start(so_pair)
    reduce_on(2, 1)

    gs_ext = ext[...].astype(BF)
    for fi in range(frames):
        z_part = lax.dot_general(
            weight((g_a, g_b), fi), gs_ext, contract_first, preferred_element_type=F32
        )
        zbuf[fi * sw : (fi + 1) * sw] = z_part[0:sw]
        if fi == 1:
            reduce_on(1, 2)
            reduce_on(2, 2)

    frame_arrived(so_pair)
    for fi in range(frames):
        piece = sof[fi * tw : fi * tw + tp]
        put((p_t,), fi, lax.dot_general(og_here, piece, contract_last, preferred_element_type=F32))
    reduce_start(0)

    def tap_sum(i, carry):
        r = pl.multiple_of(i * chunk, chunk)
        total_rows = jnp.zeros((chunk, cells), F32)
        for k in range(9):
            a, b = k // 3 - 1, k % 3 - 1
            s = a * COLUMNS + b
            rows = zbuf[pl.ds(pl.multiple_of(k * chans + r, 64), chunk)]
            rolled = pltpu.roll(rows, s % width, 1) if s else rows
            total_rows = total_rows + cut(rolled, -b)
        pre_rows = pre_ref[pl.ds(r, chunk)]
        sig = jax.nn.sigmoid(pre_rows)
        gpre_ref[pl.ds(r, chunk)] = jnp.where(
            live, total_rows * sig * (1.0 + pre_rows * (1.0 - sig)), 0.0
        )
        return carry

    lax.fori_loop(0, chans // chunk, tap_sum, 0)
    reduce_on(0, 1)
    stat = sums_start(
        1,
        [
            row_of(jnp.sum(gpre_ref[...] * normed_ref[...], axis=1, keepdims=True)),
            row_of(jnp.sum(gpre_ref[...], axis=1, keepdims=True)),
        ],
    )

    reduce_on(1, 3)
    reduce_on(2, 3)
    stat = sums_middle(1, stat)
    reduce_on(0, 2)
    reduce_on(1, 4)
    reduce_on(2, 4)
    sums = sums_end(1, stat)
    reduce_on(0, 3)

    scale = lax.rsqrt(count)
    chan_gain, chan_shift = sums[:, 0:chans], sums[:, stride : stride + chans]
    dgain[...] = scale * chan_gain
    dshift[...] = scale * chan_shift
    shift_sum = group_column(gain_row * chan_shift, group) / group_count
    gain_sum = group_column(gain_row * chan_gain, group) / group_count
    result = og[...].astype(F32) + rstd * (
        gain_column * gpre_ref[...] - shift_sum - normed_ref[...] * gain_sum
    )
    gi[...] = jnp.where(live, result, 0.0).astype(BF)

    reduce_on(0, 4)

    def finish(kind, out_stage):
        arrived(back[kind])
        block = partial[kind][c, zh, slot_own].astype(F32) + landing[4][kind][0].astype(F32)
        first, second = block[:own], block[own:]
        staged(out_stage, jnp.where(c == 0, second, first))
        return jnp.where(c == 0, first, second)

    mine, swaps = [None] * 3, [None] * 3
    ends = ((ys_t, yr_t), (ys_a, yr_a), (ys_b, yr_b))
    for kind in (1, 2, 0):
        mine[kind] = finish(kind, ends[kind][0])
        swaps[kind] = trade(1, kind, *ends[kind])
    for kind in (1, 2, 0):
        arrived(swaps[kind])
    theirs = [pair[1][0:own].astype(F32) for pair in ends]
    side_s = jnp.concatenate(mine[1:], axis=1), jnp.concatenate(theirs[1:], axis=1)
    for out, (a, b), wide in ((dws, side_s, sw), (dwt, (mine[0], theirs[0]), tw)):
        whole = jnp.concatenate([jnp.where(c == 0, a, b), jnp.where(c == 0, b, a)], axis=1)
        out[...] = scale * whole[:, 0:wide]

    for copy in pending:
        copy.wait_send()
    for pair in (og_pair, so_pair):
        frame_sent(pair)
    for pair in (act_pair, gs_pair):
        strip_sent(pair)


def hand_over(*refs):
    for source, target in zip(refs[:5], refs[5:]):
        target[...] = source[...].reshape(target.shape)


def fused(latents, out_grad, w_spatial, w_temporal, norm_gain, norm_shift, heights):
    chans, cells = latents.shape[1:]
    own, sw = w_spatial.shape
    tw = w_temporal.shape[1]
    pad = -(-own // 16) * 16
    th = -(-tw // 256) * 128
    sh = -(-sw // 256) * 128
    kinds = (th, sh - 128, 128)
    sp, tp = 2 * sh, 2 * th
    wide = -(-chans // 128) * 128

    scratch = (
        [pltpu.VMEM((2, 2, 8, 2 * own, kind), BF) for _ in range(2) for kind in kinds]
        + [
            pltpu.VMEM(lead + (2 * own, kind), BF)
            for lead in ((2, 8), (2, 4), (2, 2), (2, 1), (1,))
            for kind in kinds
        ]
        + [pltpu.VMEM((pad, kind), BF) for _ in range(4) for kind in kinds]
        + [
            pltpu.VMEM((2, chans, cells), BF),
            pltpu.VMEM((3 * chans + tp - tw, cells), BF),
            pltpu.VMEM((2, 2, chans, cells // 2), BF),
            pltpu.VMEM((2, 2, chans, cells // 2), BF),
            pltpu.VMEM((chans, 2 * cells), F32),
            pltpu.VMEM((9 * chans + sp - sw, cells), BF),
            pltpu.VMEM((9 * chans, 2 * cells), F32),
            pltpu.VMEM((chans, cells), F32),
        ]
        + [pltpu.VMEM((chans, cells), F32)] * 4
        + [
            pltpu.VMEM((2, 2, 1, 3 * wide), F32),
            pltpu.VMEM((2, 8, 1, 3 * wide), F32),
            pltpu.VMEM((2, 4, 1, 3 * wide), F32),
        ]
        + [pltpu.SemaphoreType.DMA((3, 8))] * 4
        + [pltpu.SemaphoreType.DMA((4,))] * 2
        + [pltpu.SemaphoreType.DMA((2, 2))] * 2
        + [pltpu.SemaphoreType.DMA((2, 12))] * 2
        + [pltpu.SemaphoreType.DMA((2, 3))] * 2
    )
    vmem = pl.BlockSpec(memory_space=pltpu.VMEM)
    outs = pl.pallas_call(
        whole_kernel,
        out_shape=(
            jax.ShapeDtypeStruct((chans, cells), BF),
            jax.ShapeDtypeStruct((own, sw), F32),
            jax.ShapeDtypeStruct((own, tw), F32),
            jax.ShapeDtypeStruct((1, chans), F32),
            jax.ShapeDtypeStruct((1, chans), F32),
        ),
        in_specs=[vmem] * 6 + [pl.BlockSpec(memory_space=pltpu.SMEM)],
        out_specs=(vmem,) * 5,
        scratch_shapes=scratch,
        compiler_params=pltpu.CompilerParams(
            collective_id=0, has_side_effects=True, vmem_limit_bytes=56 * 1024 * 1024
        ),
    )(
        latents[0], out_grad[0], w_spatial, w_temporal, norm_gain, norm_shift, heights
    )
    shapes = [outs[0].shape, outs[1].shape, outs[2].shape, (chans,), (chans,)]
    results = pl.pallas_call(
        hand_over,
        out_shape=tuple(
            jax.ShapeDtypeStruct(shape, out.dtype) for shape, out in zip(shapes, outs)
        ),
        in_specs=[vmem] * 5,
        out_specs=(vmem,) * 5,
    )(*outs)
    return (results[0][None],) + tuple(results[1:])


def solution(mesh):
    in_specs = (
        P("frame", None, "tile"),
        P("frame", None, "tile"),
        P("tile", "frame"),
        P("tile", "frame"),
        P(),
        P(),
        P("tile"),
    )
    out_specs = (P("frame", None, "tile"), P("tile", "frame"), P("tile", "frame"), P(), P())
    fits = mesh.shape["frame"] == 4 and mesh.shape["tile"] == 8
    return jax.shard_map(
        fused if fits else local, mesh=mesh, in_specs=in_specs, out_specs=out_specs, check_vma=False
    )
```

profile of v0, /device:TPU:0, one launch (start us, length us, event | category | flops | bytes accessed | tf_op | source)
XLA Modules:
  0.0 67.2 jit_solution(14301779397761670973)
XLA Ops:
  1.3 64.2 %shard_map.110 = (bf16[320,256]{1,0:T(8,128)(2,1)}, f32[40,720]{1,0:T(8,128)}, f32[40,240]{1,0:T(8,128)}, f32[1,320]{1,0:T(1,128)}, f32[1,320]{1,0:T(1,128)}) custom-call(bf16[320,256]{1,0:T(8,128)(2,1)} %bitcast.3, bf16[320,256]{1,0:T(8,128)(2,1)} %bitcast.4, bf16[40,720]{1,0:T(8,128)(2,1)} %ws.1, bf16[40,240]{1,0:T(8,128)(2,1)} %wt.1, f32[320]{0:T(512)} %gain.1, ...), custom_call_target="tpu_custom_call" | custom-call | tf_op jit(solution)/shard_map/pallas_call | solution.py:815
  65.5 1.7 %shard_map.111 = (bf16[320,256]{1,0:T(8,128)(2,1)}, f32[40,720]{1,0:T(8,128)}, f32[40,240]{1,0:T(8,128)}, f32[320]{0:T(512)}, f32[320]{0:T(512)}) custom-call(bf16[320,256]{1,0:T(8,128)(2,1)} %get-tuple-element.15.refs_0_, f32[40,720]{1,0:T(8,128)} %get-tuple-element.16.refs_1_, f32[40,240]{1,0:T(8,128)} %get-tuple-element.17.refs_2_, ...), custom_call_target="tpu_custom_call" | custom-call | tf_op jit(solution)/shard_map/pallas_call | solution.py:834
where the time goes:
time: 67.4 us; the launch traced here: 67.2 us
  Pallas kernels  65.9 us (98%)
  between operations  1.29 us (2%)
    pallas_call x1, Pallas kernels, fused(): pl.pallas_call(whole_kernel, out_shape=(jax.ShapeDtypeStruct((chans, cell...  64.2 us
    pallas_call x1, Pallas kernels, fused(): pl.pallas_call(hand_over, out_shape=tuple((jax.ShapeDtypeStruct(shape, ou...  1.71 us

commit v1 on v0

--- a/solution.py
+++ b/solution.py
@@ -180,24 +180,9 @@
     return lax.broadcasted_iota(jnp.int32, shape, dim)
 
 
-def row_of(column):
-    n = column.shape[0]
-    eye = iota((n, n), 0) == iota((n, n), 1)
-    return jnp.sum(jnp.where(eye, column, 0.0), axis=0, keepdims=True)
-
-
-def column_of(row):
-    n = row.shape[1]
-    eye = iota((n, n), 0) == iota((n, n), 1)
-    return jnp.sum(jnp.where(eye, row, 0.0), axis=1, keepdims=True)
-
-
-def group_column(row, size):
-    n = row.shape[1]
-    steps = 1 << 11
-    factor = steps // size + 1
-    same = (iota((n, n), 0) * factor) // steps == (iota((n, n), 1) * factor) // steps
-    return jnp.sum(jnp.where(same, row, 0.0), axis=1, keepdims=True)
+def group_of(n, size, dim):
+    factor = (1 << 11) // size + 1
+    return lax.shift_right_logical(iota((n, n), dim) * factor, 11)
 
 
 def whole_kernel(
@@ -207,7 +192,7 @@
     r0t, r0a, r0b, r1t, r1a, r1b, r2t, r2a, r2b, r3t, r3a, r3b, r4t, r4a, r4b,
     xs_t, xs_a, xs_b, xr_t, xr_a, xr_b, ys_t, ys_a, ys_b, yr_t, yr_a, yr_b,
     ogf, sof, hsend, hrecv, ext, cols, zbuf, acc, normed_ref, pre_ref, gs_ref, gpre_ref,
-    msg, tbuf, fbuf,
+    msg, tbuf, fbuf, eye_ref, same_ref,
     ag_send, ag_recv, rs_send, rs_recv, fr_send, fr_recv, ha_send, ha_recv, st_send, st_recv, tr_send, tr_recv,
 ):
     frames, tiles = 4, 8
@@ -244,6 +229,20 @@
     for d in range(1, frames):
         pl.semaphore_signal(barrier, inc=1, device_id=((f + d) % frames, t), device_id_type=MESH)
 
+    eye_ref[...] = jnp.where(iota((chans, chans), 0) == iota((chans, chans), 1), 1.0, 0.0)
+    same_ref[...] = jnp.where(
+        group_of(chans, group, 0) == group_of(chans, group, 1), 1.0, 0.0
+    )
+
+    def row_of(column):
+        return jnp.sum(eye_ref[...] * column, axis=0, keepdims=True)
+
+    def column_of(row):
+        return jnp.sum(eye_ref[...] * row, axis=1, keepdims=True)
+
+    def group_column(row):
+        return jnp.sum(same_ref[...] * row, axis=1, keepdims=True)
+
     q_own = jnp.where(zh == 0, y, x)
     p_own = jnp.where(zh == 0, x, y)
     slot_own = q_own * 4 + p_own * 2 + zl
@@ -265,6 +264,16 @@
 
     for ref, rows in zip((xs_t, xs_a, xs_b), sent):
         staged(ref, rows)
+    masked = jnp.where(live, lat[...].astype(F32), 0.0)
+    count_row = jnp.zeros((1, 128), F32) + h.astype(F32) * COLUMNS
+    own_rows = [
+        row_of(jnp.sum(masked, axis=1, keepdims=True)),
+        row_of(jnp.sum(masked * masked, axis=1, keepdims=True)),
+        count_row,
+    ]
+    gain_row = gain[...].reshape(1, chans)
+    gain_column = column_of(gain_row)
+    shift_column = column_of(shift[...].reshape(1, chans))
     pl.semaphore_wait(barrier, tiles + frames - 2)
 
     pending = []
@@ -415,6 +424,7 @@
             total = total + fbuf[which, i]
         return total
 
+    stat = sums_start(0, own_rows)
     traded = [
         trade(0, kind, src, dst)
         for kind, (src, dst) in enumerate(((xs_t, xr_t), (xs_a, xr_a), (xs_b, xr_b)))
@@ -445,17 +455,6 @@
     sof[3 * chans :] = jnp.zeros((sof.shape[0] - 3 * chans, cells), BF)
     cols[9 * chans :] = jnp.zeros((cols.shape[0] - 9 * chans, cells), BF)
 
-    lat32 = lat[...].astype(F32)
-    masked = jnp.where(live, lat32, 0.0)
-    count_row = jnp.zeros((1, 128), F32) + h.astype(F32) * COLUMNS
-    stat = sums_start(
-        0,
-        [
-            row_of(jnp.sum(masked, axis=1, keepdims=True)),
-            row_of(jnp.sum(masked * masked, axis=1, keepdims=True)),
-            count_row,
-        ],
-    )
     chain = [None] * 3
     for kind, ref in enumerate((xr_t, xr_a, xr_b)):
         arrived(traded[kind])
@@ -470,20 +469,14 @@
         if step < 5:
             chain[kind] = gather_step(kind, step)
 
+    stat = sums_middle(0, stat)
     forth(0, 1)
-    stat = sums_middle(0, stat)
-    forth(1, 1)
-    forth(2, 1)
-    forth(0, 2)
     total = sums_end(0, stat)
     count = total[:, 2 * stride : 2 * stride + 1]
     group_count = count * group
-    gain_row = gain[...].reshape(1, chans)
-    gain_column = column_of(gain_row)
-    shift_column = column_of(shift[...].reshape(1, chans))
-    mean = group_column(total[:, 0:chans], group) / group_count
+    mean = group_column(total[:, 0:chans]) / group_count
     rstd = lax.rsqrt(
-        group_column(total[:, stride : stride + chans], group) / group_count - mean * mean + EPSILON
+        group_column(total[:, stride : stride + chans]) / group_count - mean * mean + EPSILON
     )
     normed = (lat[...].astype(F32) - mean) * rstd
     pre = gain_column * normed + shift_column
@@ -492,16 +485,16 @@
     act = jnp.where(live, pre * jax.nn.sigmoid(pre), 0.0).astype(BF).astype(F32)
     act_pair = strip_copies(0)
     strip_start(act_pair, 0, act)
-    forth(1, 2)
-    forth(0, 3)
-    forth(2, 2)
+    forth(1, 1)
+    forth(2, 1)
+    forth(0, 2)
     frame_arrived(og_pair)
     og_here = jnp.where(live, og[...], jnp.zeros((), BF))
     og_next = jnp.where(live, ogf[1], jnp.zeros((), BF))
     og_prev = jnp.where(live, ogf[0], jnp.zeros((), BF))
-    forth(1, 3)
-    forth(0, 4)
-    forth(2, 3)
+    forth(1, 2)
+    forth(2, 2)
+    forth(0, 3)
     strip_arrived(act_pair)
     ext[...] = strip_extended(0, act)
 
@@ -530,7 +523,11 @@
             cols[pl.ds(pl.multiple_of(k * chans + r, 64), chunk)] = cut(rolled, b).astype(BF)
         return carry
 
-    lax.fori_loop(0, chans // chunk, tap_rows, 0)
+    lax.fori_loop(0, 2, tap_rows, 0)
+    forth(0, 4)
+    forth(1, 3)
+    lax.fori_loop(2, chans // chunk, tap_rows, 0)
+    forth(2, 3)
 
     def slots(fi):
         yi, xi = fi // 2, fi % 2
@@ -568,13 +565,12 @@
     for fi in range(frames):
         block = weight((g_t,), fi)
         lo, hi = fi * tw, (fi + 1) * tw
-        for k in range(3):
+        taps = [k for k in range(3) if max(lo, k * chans) < min(hi, (k + 1) * chans)]
+        window = jnp.concatenate([windows[k] for k in taps], axis=1)
+        part = lax.dot_general(block, window, contract_first, preferred_element_type=F32)
+        for i, k in enumerate(taps):
             first, last = max(lo, k * chans), min(hi, (k + 1) * chans)
-            if first < last:
-                part = lax.dot_general(
-                    block, windows[k], contract_first, preferred_element_type=F32
-                )
-                zbuf[first:last, 0:cells] = part[first - lo : last - lo]
+            zbuf[first:last, 0:cells] = part[first - lo : last - lo, i * cells : (i + 1) * cells]
     gs = zbuf[0:chans, 0:cells] + zbuf[chans : 2 * chans, 0:cells]
     gs = gs + zbuf[2 * chans : 3 * chans, 0:cells]
     gs = jnp.where(live, gs, 0.0).astype(BF).astype(F32)
@@ -705,8 +701,18 @@
         )
         return carry
 
-    lax.fori_loop(0, chans // chunk, tap_sum, 0)
+    lax.fori_loop(0, 1, tap_sum, 0)
     reduce_on(0, 1)
+    lax.fori_loop(1, 2, tap_sum, 0)
+    reduce_on(1, 3)
+    reduce_on(2, 3)
+    lax.fori_loop(2, 3, tap_sum, 0)
+    reduce_on(0, 2)
+    lax.fori_loop(3, 4, tap_sum, 0)
+    reduce_on(1, 4)
+    reduce_on(2, 4)
+    lax.fori_loop(4, chans // chunk, tap_sum, 0)
+    reduce_on(0, 3)
     stat = sums_start(
         1,
         [
@@ -715,28 +721,6 @@
         ],
     )
 
-    reduce_on(1, 3)
-    reduce_on(2, 3)
-    stat = sums_middle(1, stat)
-    reduce_on(0, 2)
-    reduce_on(1, 4)
-    reduce_on(2, 4)
-    sums = sums_end(1, stat)
-    reduce_on(0, 3)
-
-    scale = lax.rsqrt(count)
-    chan_gain, chan_shift = sums[:, 0:chans], sums[:, stride : stride + chans]
-    dgain[...] = scale * chan_gain
-    dshift[...] = scale * chan_shift
-    shift_sum = group_column(gain_row * chan_shift, group) / group_count
-    gain_sum = group_column(gain_row * chan_gain, group) / group_count
-    result = og[...].astype(F32) + rstd * (
-        gain_column * gpre_ref[...] - shift_sum - normed_ref[...] * gain_sum
-    )
-    gi[...] = jnp.where(live, result, 0.0).astype(BF)
-
-    reduce_on(0, 4)
-
     def finish(kind, out_stage):
         arrived(back[kind])
         block = partial[kind][c, zh, slot_own].astype(F32) + landing[4][kind][0].astype(F32)
@@ -746,9 +730,26 @@
 
     mine, swaps = [None] * 3, [None] * 3
     ends = ((ys_t, yr_t), (ys_a, yr_a), (ys_b, yr_b))
-    for kind in (1, 2, 0):
+    for kind in (1, 2):
         mine[kind] = finish(kind, ends[kind][0])
         swaps[kind] = trade(1, kind, *ends[kind])
+    stat = sums_middle(1, stat)
+    reduce_on(0, 4)
+    sums = sums_end(1, stat)
+
+    scale = lax.rsqrt(count)
+    chan_gain, chan_shift = sums[:, 0:chans], sums[:, stride : stride + chans]
+    dgain[...] = scale * chan_gain
+    dshift[...] = scale * chan_shift
+    shift_sum = group_column(gain_row * chan_shift) / group_count
+    gain_sum = group_column(gain_row * chan_gain) / group_count
+    result = og[...].astype(F32) + rstd * (
+        gain_column * gpre_ref[...] - shift_sum - normed_ref[...] * gain_sum
+    )
+    gi[...] = jnp.where(live, result, 0.0).astype(BF)
+
+    mine[0] = finish(0, ends[0][0])
+    swaps[0] = trade(1, 0, *ends[0])
     for kind in (1, 2, 0):
         arrived(swaps[kind])
     theirs = [pair[1][0:own].astype(F32) for pair in ends]
@@ -804,6 +805,8 @@
             pltpu.VMEM((2, 2, 1, 3 * wide), F32),
             pltpu.VMEM((2, 8, 1, 3 * wide), F32),
             pltpu.VMEM((2, 4, 1, 3 * wide), F32),
+            pltpu.VMEM((chans, chans), F32),
+            pltpu.VMEM((chans, chans), F32),
         ]
         + [pltpu.SemaphoreType.DMA((3, 8))] * 4
         + [pltpu.SemaphoreType.DMA((4,))] * 2

time: 67.4 us -> 72.7 us (1.079)
  Pallas kernels: 65.9 us -> 71.1 us
    pallas_call x1, Pallas kernels: 64.2 us -> 69.4 us  [fused(): pl.pallas_call(whole_kernel, out_shape=(jax.ShapeDtypeStruct((chans, cell...]
where the time goes in v1:
time: 72.7 us; the launch traced here: 72.4 us
  Pallas kernels  71.1 us (98%)
  between operations  1.29 us (2%)
    pallas_call x1, Pallas kernels, fused(): pl.pallas_call(whole_kernel, out_shape=(jax.ShapeDtypeStruct((chans, cell...  69.4 us
    pallas_call x1, Pallas kernels, fused(): pl.pallas_call(hand_over, out_shape=tuple((jax.ShapeDtypeStruct(shape, ou...  1.71 us

profile of v1, /device:TPU:0, one launch (start us, length us, event | category | flops | bytes accessed | tf_op | source)
XLA Modules:
  0.0 72.4 jit_solution(9209422975394144731)
XLA Ops:
  1.3 69.4 %shard_map.110 = (bf16[320,256]{1,0:T(8,128)(2,1)}, f32[40,720]{1,0:T(8,128)}, f32[40,240]{1,0:T(8,128)}, f32[1,320]{1,0:T(1,128)}, f32[1,320]{1,0:T(1,128)}) custom-call(bf16[320,256]{1,0:T(8,128)(2,1)} %bitcast.3, bf16[320,256]{1,0:T(8,128)(2,1)} %bitcast.4, bf16[40,720]{1,0:T(8,128)(2,1)} %ws.1, bf16[40,240]{1,0:T(8,128)(2,1)} %wt.1, f32[320]{0:T(512)} %gain.1, ...), custom_call_target="tpu_custom_call" | custom-call | tf_op jit(solution)/shard_map/pallas_call | solution.py:818
  70.7 1.7 %shard_map.111 = (bf16[320,256]{1,0:T(8,128)(2,1)}, f32[40,720]{1,0:T(8,128)}, f32[40,240]{1,0:T(8,128)}, f32[320]{0:T(512)}, f32[320]{0:T(512)}) custom-call(bf16[320,256]{1,0:T(8,128)(2,1)} %get-tuple-element.15.refs_0_, f32[40,720]{1,0:T(8,128)} %get-tuple-element.16.refs_1_, f32[40,240]{1,0:T(8,128)} %get-tuple-element.17.refs_2_, ...), custom_call_target="tpu_custom_call" | custom-call | tf_op jit(solution)/shard_map/pallas_call | solution.py:837

commit v2 on v1

--- a/solution.py
+++ b/solution.py
@@ -435,12 +435,10 @@
     @pl.when(f == 0)
     def _():
         ogf[0] = jnp.zeros_like(ogf[0])
-        sof[0:chans] = jnp.zeros((chans, cells), BF)
 
     @pl.when(f == frames - 1)
     def _():
         ogf[1] = jnp.zeros_like(ogf[1])
-        sof[2 * chans : 3 * chans] = jnp.zeros((chans, cells), BF)
 
     @pl.when(t == 0)
     def _():
@@ -469,8 +467,11 @@
         if step < 5:
             chain[kind] = gather_step(kind, step)
 
+    forth(0, 1)
     stat = sums_middle(0, stat)
-    forth(0, 1)
+    forth(1, 1)
+    forth(2, 1)
+    forth(0, 2)
     total = sums_end(0, stat)
     count = total[:, 2 * stride : 2 * stride + 1]
     group_count = count * group
@@ -485,16 +486,15 @@
     act = jnp.where(live, pre * jax.nn.sigmoid(pre), 0.0).astype(BF).astype(F32)
     act_pair = strip_copies(0)
     strip_start(act_pair, 0, act)
-    forth(1, 1)
-    forth(2, 1)
-    forth(0, 2)
+    forth(1, 2)
+    forth(0, 3)
+    forth(2, 2)
     frame_arrived(og_pair)
     og_here = jnp.where(live, og[...], jnp.zeros((), BF))
     og_next = jnp.where(live, ogf[1], jnp.zeros((), BF))
     og_prev = jnp.where(live, ogf[0], jnp.zeros((), BF))
-    forth(1, 2)
-    forth(2, 2)
-    forth(0, 3)
+    forth(1, 3)
+    forth(0, 4)
     strip_arrived(act_pair)
     ext[...] = strip_extended(0, act)
 
@@ -523,11 +523,9 @@
             cols[pl.ds(pl.multiple_of(k * chans + r, 64), chunk)] = cut(rolled, b).astype(BF)
         return carry
 
-    lax.fori_loop(0, 2, tap_rows, 0)
-    forth(0, 4)
-    forth(1, 3)
-    lax.fori_loop(2, chans // chunk, tap_rows, 0)
+    lax.fori_loop(0, 1, tap_rows, 0)
     forth(2, 3)
+    lax.fori_loop(1, chans // chunk, tap_rows, 0)
 
     def slots(fi):
         yi, xi = fi // 2, fi % 2
@@ -584,7 +582,10 @@
         put((p_a, p_b), fi, lax.dot_general(here, piece, contract_last, preferred_element_type=F32))
         return carry
 
-    lax.fori_loop(0, frames, spatial_terms, 0)
+    forth(1, 4)
+    lax.fori_loop(0, 2, spatial_terms, 0)
+    forth(2, 4)
+    lax.fori_loop(2, frames, spatial_terms, 0)
 
     def reduce_step(kind, step):
         buf = partial[kind]
@@ -643,8 +644,6 @@
         reduce_add(kind, step - 1)
         back[kind] = reduce_step(kind, step)
 
-    forth(1, 4)
-    forth(2, 4)
     reduce_start(1)
     reduce_start(2)
     strip_arrived(gs_pair)
@@ -662,11 +661,24 @@
 
     lax.fori_loop(0, frames, forward, 0)
     spatial_out = jnp.where(live, acc[...], 0.0).astype(BF)
-    sof[chans : 2 * chans] = spatial_out
-    so_pair = frame_copies(
-        sof.at[pl.ds(chans, chans)], sof.at[pl.ds(0, chans)], sof.at[pl.ds(2 * chans, chans)], 2
-    )
-    frame_start(so_pair)
+    for k in range(3):
+        sof[k * chans : (k + 1) * chans] = spatial_out
+
+    for fi in range(frames):
+        lo, hi = fi * tw, (fi + 1) * tw
+        piece = sof[lo : lo + tp]
+        value = None
+        for k in range(3):
+            if max(lo, k * chans) < min(hi, (k + 1) * chans):
+                term = lax.dot_general(
+                    windows[k], piece, contract_last, preferred_element_type=F32
+                )
+                if value is None:
+                    value = term
+                else:
+                    value = jnp.where(iota((1, tp), 1) < k * chans - lo, value, term)
+        put((p_t,), fi, value)
+    reduce_start(0)
     reduce_on(2, 1)
 
     gs_ext = ext[...].astype(BF)
@@ -677,13 +689,8 @@
         zbuf[fi * sw : (fi + 1) * sw] = z_part[0:sw]
         if fi == 1:
             reduce_on(1, 2)
+            reduce_on(0, 1)
             reduce_on(2, 2)
-
-    frame_arrived(so_pair)
-    for fi in range(frames):
-        piece = sof[fi * tw : fi * tw + tp]
-        put((p_t,), fi, lax.dot_general(og_here, piece, contract_last, preferred_element_type=F32))
-    reduce_start(0)
 
     def tap_sum(i, carry):
         r = pl.multiple_of(i * chunk, chunk)
@@ -701,18 +708,16 @@
         )
         return carry
 
+    reduce_on(0, 2)
     lax.fori_loop(0, 1, tap_sum, 0)
-    reduce_on(0, 1)
-    lax.fori_loop(1, 2, tap_sum, 0)
     reduce_on(1, 3)
     reduce_on(2, 3)
-    lax.fori_loop(2, 3, tap_sum, 0)
-    reduce_on(0, 2)
-    lax.fori_loop(3, 4, tap_sum, 0)
+    reduce_on(0, 3)
+    lax.fori_loop(1, 3, tap_sum, 0)
     reduce_on(1, 4)
     reduce_on(2, 4)
-    lax.fori_loop(4, chans // chunk, tap_sum, 0)
-    reduce_on(0, 3)
+    reduce_on(0, 4)
+    lax.fori_loop(3, chans // chunk, tap_sum, 0)
     stat = sums_start(
         1,
         [
@@ -734,7 +739,8 @@
         mine[kind] = finish(kind, ends[kind][0])
         swaps[kind] = trade(1, kind, *ends[kind])
     stat = sums_middle(1, stat)
-    reduce_on(0, 4)
+    mine[0] = finish(0, ends[0][0])
+    swaps[0] = trade(1, 0, *ends[0])
     sums = sums_end(1, stat)
 
     scale = lax.rsqrt(count)
@@ -748,8 +754,6 @@
     )
     gi[...] = jnp.where(live, result, 0.0).astype(BF)
 
-    mine[0] = finish(0, ends[0][0])
-    swaps[0] = trade(1, 0, *ends[0])
     for kind in (1, 2, 0):
         arrived(swaps[kind])
     theirs = [pair[1][0:own].astype(F32) for pair in ends]
@@ -760,8 +764,7 @@
 
     for copy in pending:
         copy.wait_send()
-    for pair in (og_pair, so_pair):
-        frame_sent(pair)
+    frame_sent(og_pair)
     for pair in (act_pair, gs_pair):
         strip_sent(pair)
 
@@ -809,7 +812,7 @@
             pltpu.VMEM((chans, chans), F32),
         ]
         + [pltpu.SemaphoreType.DMA((3, 8))] * 4
-        + [pltpu.SemaphoreType.DMA((4,))] * 2
+        + [pltpu.SemaphoreType.DMA((2,))] * 2
         + [pltpu.SemaphoreType.DMA((2, 2))] * 2
         + [pltpu.SemaphoreType.DMA((2, 12))] * 2
         + [pltpu.SemaphoreType.DMA((2, 3))] * 2

time: 72.7 us -> 61.5 us (0.85)
  Pallas kernels: 71.1 us -> 60.1 us
    pallas_call x1, Pallas kernels: 69.4 us -> 58.4 us  [fused(): pl.pallas_call(whole_kernel, out_shape=(jax.ShapeDtypeStruct((chans, cell...]
where the time goes in v2:
time: 61.5 us; the launch traced here: 61.4 us
  Pallas kernels  60.1 us (98%)
  between operations  1.29 us (2%)
    pallas_call x1, Pallas kernels, fused(): pl.pallas_call(whole_kernel, out_shape=(jax.ShapeDtypeStruct((chans, cell...  58.4 us
    pallas_call x1, Pallas kernels, fused(): pl.pallas_call(hand_over, out_shape=tuple((jax.ShapeDtypeStruct(shape, ou...  1.71 us

profile of v2, /device:TPU:0, one launch (start us, length us, event | category | flops | bytes accessed | tf_op | source)
XLA Modules:
  0.0 61.4 jit_solution(9830518146639927643)
XLA Ops:
  1.3 58.4 %shard_map.110 = (bf16[320,256]{1,0:T(8,128)(2,1)}, f32[40,720]{1,0:T(8,128)}, f32[40,240]{1,0:T(8,128)}, f32[1,320]{1,0:T(1,128)}, f32[1,320]{1,0:T(1,128)}) custom-call(bf16[320,256]{1,0:T(8,128)(2,1)} %bitcast.3, bf16[320,256]{1,0:T(8,128)(2,1)} %bitcast.4, bf16[40,720]{1,0:T(8,128)(2,1)} %ws.1, bf16[40,240]{1,0:T(8,128)(2,1)} %wt.1, f32[320]{0:T(512)} %gain.1, ...), custom_call_target="tpu_custom_call" | custom-call | tf_op jit(solution)/shard_map/pallas_call | solution.py:821
  59.6 1.7 %shard_map.111 = (bf16[320,256]{1,0:T(8,128)(2,1)}, f32[40,720]{1,0:T(8,128)}, f32[40,240]{1,0:T(8,128)}, f32[320]{0:T(512)}, f32[320]{0:T(512)}) custom-call(bf16[320,256]{1,0:T(8,128)(2,1)} %get-tuple-element.15.refs_0_, f32[40,720]{1,0:T(8,128)} %get-tuple-element.16.refs_1_, f32[40,240]{1,0:T(8,128)} %get-tuple-element.17.refs_2_, ...), custom_call_target="tpu_custom_call" | custom-call | tf_op jit(solution)/shard_map/pallas_call | solution.py:840

commit v3 on v2

--- a/solution.py
+++ b/solution.py
@@ -489,10 +489,6 @@
     forth(1, 2)
     forth(0, 3)
     forth(2, 2)
-    frame_arrived(og_pair)
-    og_here = jnp.where(live, og[...], jnp.zeros((), BF))
-    og_next = jnp.where(live, ogf[1], jnp.zeros((), BF))
-    og_prev = jnp.where(live, ogf[0], jnp.zeros((), BF))
     forth(1, 3)
     forth(0, 4)
     strip_arrived(act_pair)
@@ -558,6 +554,10 @@
     contract_first = (((0,), (0,)), ((), ()))
     contract_last = (((1,), (1,)), ((), ()))
 
+    frame_arrived(og_pair)
+    og_here = jnp.where(live, og[...], jnp.zeros((), BF))
+    og_next = jnp.where(live, ogf[1], jnp.zeros((), BF))
+    og_prev = jnp.where(live, ogf[0], jnp.zeros((), BF))
     forth(0, 5)
     windows = (og_next, og_here, og_prev)
     for fi in range(frames):

time: 61.5 us -> 61.5 us (level)
  no operation moved by 1% of the time
where the time goes in v3:
time: 61.5 us; the launch traced here: 61.4 us
  Pallas kernels  60.1 us (98%)
  between operations  1.29 us (2%)
    pallas_call x1, Pallas kernels, fused(): pl.pallas_call(whole_kernel, out_shape=(jax.ShapeDtypeStruct((chans, cell...  58.4 us
    pallas_call x1, Pallas kernels, fused(): pl.pallas_call(hand_over, out_shape=tuple((jax.ShapeDtypeStruct(shape, ou...  1.71 us

profile of v3, /device:TPU:0, one launch (start us, length us, event | category | flops | bytes accessed | tf_op | source)
XLA Modules:
  0.0 61.4 jit_solution(17923440406485211065)
XLA Ops:
  1.3 58.4 %shard_map.110 = (bf16[320,256]{1,0:T(8,128)(2,1)}, f32[40,720]{1,0:T(8,128)}, f32[40,240]{1,0:T(8,128)}, f32[1,320]{1,0:T(1,128)}, f32[1,320]{1,0:T(1,128)}) custom-call(bf16[320,256]{1,0:T(8,128)(2,1)} %bitcast.3, bf16[320,256]{1,0:T(8,128)(2,1)} %bitcast.4, bf16[40,720]{1,0:T(8,128)(2,1)} %ws.1, bf16[40,240]{1,0:T(8,128)(2,1)} %wt.1, f32[320]{0:T(512)} %gain.1, ...), custom_call_target="tpu_custom_call" | custom-call | tf_op jit(solution)/shard_map/pallas_call | solution.py:821
  59.6 1.7 %shard_map.111 = (bf16[320,256]{1,0:T(8,128)(2,1)}, f32[40,720]{1,0:T(8,128)}, f32[40,240]{1,0:T(8,128)}, f32[320]{0:T(512)}, f32[320]{0:T(512)}) custom-call(bf16[320,256]{1,0:T(8,128)(2,1)} %get-tuple-element.15.refs_0_, f32[40,720]{1,0:T(8,128)} %get-tuple-element.16.refs_1_, f32[40,240]{1,0:T(8,128)} %get-tuple-element.17.refs_2_, ...), custom_call_target="tpu_custom_call" | custom-call | tf_op jit(solution)/shard_map/pallas_call | solution.py:840
